TPU v7x, 32 devices: a whole 2x2x4 slice. The times are simulated.
32 devices in a mesh: fsdp: 4 (over y, x), rep: 8 (over z, core).
Axes of the slice: x: 2, y: 2, z: 4, core: 2. Of those that a mesh axis runs over, the one named last changes fastest.
Arguments:
- grads: bfloat16 [4, 8, 2, 512, 512], P('fsdp', 'rep'), may hold values from -0.25 to 0.25
- targets: int32 [4, 8, 2], P(None, 'rep'), may hold values from 0 to 7, as said below
- left_factor: float32 [4, 8, 2, 512, 512], P('fsdp', 'rep'), as said below
- right_factor: float32 [4, 8, 2, 512, 512], P('fsdp', 'rep'), as said below
- left_root: bfloat16 [4, 8, 2, 512, 512], P('fsdp', 'rep'), as said below
- right_root: bfloat16 [4, 8, 2, 512, 512], P('fsdp', 'rep'), as said below
- refresh: int32 [4, 8, 2], P('fsdp', 'rep'), may hold values 0 or 1
- buddy_offset: int32 [4], P('fsdp'), may hold values from 1 to 7
Outputs:
- new_left: bfloat16 [4, 8, 2, 512, 512], P('fsdp', 'rep')
- new_right: bfloat16 [4, 8, 2, 512, 512], P('fsdp', 'rep')
- buddy_left: bfloat16 [4, 8, 2, 512, 512], P('fsdp', 'rep')
- buddy_right: bfloat16 [4, 8, 2, 512, 512], P('fsdp', 'rep')
- precond: bfloat16 [4, 8, 2, 512, 512], P('fsdp', 'rep')
Inputs may be any that keep to these rules, and one draw needn't show every extreme that they name: `targets`: for each replica index r, the blocks (f, r, k) fill every (owner, slot) pair exactly once; one device sends at most 1 block to one owner, and some device does so. `left_factor`: symmetric and positive definite. `right_factor`: symmetric and positive definite. `left_root`: symmetric. `right_root`: symmetric.
All inputs are finite; a program needn't handle non-finite values. No bound on the sum of `refresh` on one device may be relied on, other than what follows from the above.
Results may differ from a plain program's by a relative error of at most 0.0057.
Values may be sent and summed in bfloat16 or wider, within the bound.
A program may use at most 128 MiB of HBM per device.

v0:
```python
import jax
import jax.numpy as jnp
from jax import lax
from jax.sharding import PartitionSpec as P


def partner(value, axis, bit):
    mask = 2**bit
    pairs = [(source, source ^ mask) for source in range(lax.axis_size(axis))]
    return lax.ppermute(value, axis, pairs)


def batched(left, right):
    return jnp.einsum("kab,kbc->kac", left, right, precision=lax.Precision.HIGHEST)


def refine(factor, root):
    square = batched(root, root)
    fourth = batched(square, square)
    moment = batched(fourth, factor)
    return (5.0 * root - batched(root, moment)) / 4.0


def precondition(owned, left_factor, right_factor, left_root, right_root, refresh):
    lfac = left_factor + jnp.einsum(
        "kab,kcb->kac", owned, owned, preferred_element_type=jnp.float32
    )
    rfac = right_factor + jnp.einsum(
        "kba,kbc->kac", owned, owned, preferred_element_type=jnp.float32
    )
    lold = left_root.astype(jnp.float32)
    rold = right_root.astype(jnp.float32)
    flag = (refresh == 1)[:, None, None]
    lnew = jnp.where(flag, refine(lfac, lold), lold).astype(jnp.bfloat16)
    rnew = jnp.where(flag, refine(rfac, rold), rold).astype(jnp.bfloat16)
    half = jnp.einsum("kab,kbc->kac", lnew, owned, preferred_element_type=jnp.float32).astype(
        jnp.bfloat16
    )
    result = jnp.einsum("kab,kbc->kac", half, rnew, preferred_element_type=jnp.float32).astype(
        jnp.bfloat16
    )
    return (lnew, rnew, result)


def cross_level(copies, level):
    return partner((copies[0], copies[1]), "rep", level)


def per_device(
    grads, targets, left_factor, right_factor, left_root, right_root, refresh, buddy_offset
):
    groups = lax.axis_size("fsdp")
    myself = lax.axis_index("fsdp")
    per_dev = grads.shape[2]
    width = grads.shape[3]
    table = targets[:, 0, :]
    owner = table // per_dev
    slot = table % per_dev
    slot_ids = jnp.arange(per_dev, dtype=jnp.int32)
    mine = owner == myself
    everyone = lax.all_gather(grads, "fsdp", axis=0, tiled=True).reshape(
        groups * per_dev, width, width
    )
    pick = jnp.logical_and(mine[None], slot[None] == slot_ids[:, None, None])
    pick = pick.reshape(per_dev, groups * per_dev).astype(jnp.bfloat16)
    owned = jnp.einsum("sj,jab->sab", pick, everyone, preferred_element_type=jnp.float32).astype(
        jnp.bfloat16
    )
    lnew, rnew, result = precondition(
        owned,
        left_factor[0, 0],
        right_factor[0, 0],
        left_root[0, 0],
        right_root[0, 0],
        refresh[0, 0],
    )
    collected = lax.all_gather(result[None, None], "fsdp", axis=0, tiled=True).reshape(
        groups * per_dev, width, width
    )
    my_targets = lax.dynamic_index_in_dim(table, myself, 0, keepdims=False)
    home_pick = (
        jnp.arange(groups * per_dev, dtype=jnp.int32)[None, :] == my_targets[:, None]
    ).astype(jnp.bfloat16)
    precond = jnp.einsum(
        "kj,jab->kab", home_pick, collected, preferred_element_type=jnp.float32
    ).astype(jnp.bfloat16)
    levels = lax.axis_size("rep").bit_length() - 1
    sequence = range(levels)
    copies = (lnew, rnew)
    for level in sequence:
        crossing = jnp.bitwise_and(jnp.right_shift(buddy_offset[0], level), 1) == 1
        moved = cross_level(copies, level)
        copies = (
            jnp.where(crossing, moved[0], copies[0]),
            jnp.where(crossing, moved[1], copies[1]),
        )
    shape = grads.shape
    return (
        lnew.reshape(shape),
        rnew.reshape(shape),
        copies[0].reshape(shape),
        copies[1].reshape(shape),
        precond.reshape(shape),
    )


def solution(mesh):
    placed = (
        P("fsdp", "rep", None, None, None),
        P(None, "rep", None),
        P("fsdp", "rep", None, None, None),
        P("fsdp", "rep", None, None, None),
        P("fsdp", "rep", None, None, None),
        P("fsdp", "rep", None, None, None),
        P("fsdp", "rep", None),
        P("fsdp"),
    )
    return jax.shard_map(
        per_device,
        mesh=mesh,
        in_specs=placed,
        out_specs=(
            P("fsdp", "rep", None, None, None),
            P("fsdp", "rep", None, None, None),
            P("fsdp", "rep", None, None, None),
            P("fsdp", "rep", None, None, None),
            P("fsdp", "rep", None, None, None),
        ),
        check_vma=False,
    )
```

profile of v0, /device:TPU:0, one launch (start us, length us, event | category | flops | bytes accessed | tf_op | source)
XLA Modules:
  0.0 224.5 jit_solution(14200239756988491619)
XLA Ops:
  8.0 0.8 copy.38
  8.8 2.4 %copy.35 = bf16[1,1,2,512,512]{3,4,2,1,0:T(8,128)(2,1)} copy(bf16[1,1,2,512,512]{4,3,2,1,0:T(8,128)(2,1)} %param.12) | data formatting | bytes 2097152 | tf_op args[4]
  11.2 1.3 copy.44
  14.0 4.9 %fusion.44 = f32[2,512,512]{2,1,0:T(8,128)} fusion(f32[2,512,512]{2,1,0:T(8,128)S(1)} %fusion.24), kind=kOutput, calls=%fused_computation.58 | convolution fusion | flops 3221225472 | bytes 4194304 | tf_op jit(solution)/shard_map/kab,kbc->kac/dot_general | solution.py:14
  18.8 3.5 %fusion.45 = f32[2,512,512]{2,1,0:T(8,128)S(1)} fusion(f32[2,512,512]{2,1,0:T(8,128)S(1)} %fusion.21), kind=kOutput, calls=%fused_computation.59 | convolution fusion | flops 3221225472 | bytes 4194304 | tf_op jit(solution)/shard_map/kab,kbc->kac/dot_general | solution.py:14
  22.4 42.9 %all-gather.4.cloned.1.call-done = bf16[4,1,2,512,512]{4,3,2,1,0:T(8,128)(2,1)} async-done(((bf16[1,1,2,512,512]{4,3,2,1,0:T(8,128)(2,1)}), bf16[4,1,2,512,512]{4,3,2,1,0:T(8,128)(2,1)}) %all-gather.4.cloned.1.call-update) | async-done | bytes 4194320 | tf_op jit(solution)/shard_map/all_gather | solution.py:61
  65.3 5.0 %fusion.15 = bf16[2,512,512]{2,0,1:T(2,128)(2,1)S(1)} fusion(bf16[8,512,512]{2,1,0:T(8,128)(2,1)} %bitcast.60, pred[8]{0:T(512)(128)(4,1)S(1)} %fusion.43, s32[8]{0:T(128)S(1)} %and_select_fusion), kind=kOutput, calls=%fused_computation.19 | convolution fusion | flops 8912928 | bytes 5242920 | tf_op jit(solution)/shard_map/sj,jab->sab/dot_general | solution.py:66
  70.3 0.8 fusion.31
  71.0 0.8 fusion.29
  71.8 0.9 copy-done
  72.8 3.8 %fusion.11 = f32[2,512,512]{1,2,0:T(8,128)S(1)} fusion(f32[2,512,512]{2,1,0:T(8,128)S(1)} %copy-done, f32[2,512,512]{2,1,0:T(8,128)S(1)} %fusion.31, f32[1,1,2,512,512]{4,3,2,1,0:T(8,128)S(1)} %copy-done.6), kind=kOutput, calls=%fused_computation.17 | convolution fusion | flops 3221749760 | bytes 8388608 | tf_op jit(solution)/shard_map/kab,kbc->kac/dot_general | solution.py:14
  76.6 3.0 %fusion.6 = bf16[2,512,512]{1,2,0:T(8,128)(2,1)} fusion(f32[2,512,512]{1,2,0:T(8,128)S(1)} %fusion.11, bf16[1,1,2,512,512]{4,3,2,1,0:T(8,128)(2,1)S(1)} %copy-done.2, bf16[1,1,2,512,512]{3,4,2,1,0:T(8,128)(2,1)S(1)} %copy-done.9, pred[2]{0:T(512)(128)(4,1)S(1)} %compare_bitcast_fusion), kind=kOutput, calls=%fused_computation.10 | convolution fusion | flops 3224371200 | bytes 5242882 | tf_op jit(solution)/shard_map/kab,kbc->kac/dot_general | solution.py:14
  79.6 3.6 %fusion.10 = f32[2,512,512]{1,2,0:T(8,128)S(1)} fusion(f32[2,512,512]{2,1,0:T(8,128)S(1)} %fusion.45, f32[2,512,512]{2,1,0:T(8,128)S(1)} %fusion.29, f32[1,1,2,512,512]{4,3,2,1,0:T(8,128)S(1)} %copy-done.7), kind=kOutput, calls=%fused_computation.15 | convolution fusion | flops 3221749760 | bytes 8388608 | tf_op jit(solution)/shard_map/kab,kbc->kac/dot_general | solution.py:14
  83.3 2.1 fusion.9
  85.4 2.3 %convolution_convert_fusion = bf16[2,512,512]{2,1,0:T(8,128)(2,1)} fusion(bf16[2,512,512]{1,2,0:T(8,128)(2,1)S(1)} %fusion.9, bf16[2,512,512]{1,2,0:T(8,128)(2,1)S(1)} %copy-done.5, bf16[2,512,512]{2,0,1:T(2,128)(2,1)S(1)} %fusion.15), kind=kOutput, calls=%fused_computation.20 | convolution fusion | flops 1074790400 | bytes 4194304 | tf_op jit(solution)/shard_map/kab,kbc->kac/dot_general | solution.py:39
  88.9 1.5 collective-permute-done
  90.6 1.6 collective-permute-start.1
  92.3 1.4 collective-permute-start.4
  93.6 23.0 %collective-permute-done.1 = bf16[2,512,512]{1,2,0:T(8,128)(2,1)S(1)} collective-permute-done((bf16[2,512,512]{1,2,0:T(8,128)(2,1)S(1)}, bf16[2,512,512]{1,2,0:T(8,128)(2,1)S(1)}, u32[]{:S(2)}, u32[]{:S(2)}) %collective-permute-start.1) | collective-permute-done | bytes 1048608 | tf_op jit(solution)/shard_map/ppermute | solution.py:10
  116.8 2.5 %collective-permute-start.2 = (bf16[2,512,512]{1,2,0:T(8,128)(2,1)S(1)}, bf16[2,512,512]{1,2,0:T(8,128)(2,1)}, u32[]{:S(2)}, u32[]{:S(2)}) collective-permute-start(bf16[2,512,512]{1,2,0:T(8,128)(2,1)S(1)} %broadcast_select_fusion.3), channel_id=1, source_target_pairs={{0,4},{1,5},{2,6},{3,7},{4,0},{5,1},{6,2},{7,3},{8,12},{9,13},{10,... | collective-permute-start | bytes 3145736 | tf_op jit(solution)/shard_map/ppermute | solution.py:10
  119.2 40.5 %collective-permute-done.4 = bf16[2,512,512]{1,2,0:T(8,128)(2,1)S(1)} collective-permute-done((bf16[2,512,512]{1,2,0:T(8,128)(2,1)S(1)}, bf16[2,512,512]{1,2,0:T(8,128)(2,1)S(1)}, u32[]{:S(2)}, u32[]{:S(2)}) %collective-permute-start.4) | collective-permute-done | bytes 1048608 | tf_op jit(solution)/shard_map/ppermute | solution.py:10
  159.7 1.1 broadcast_select_fusion.2
  160.9 1.3 copy.55
  162.3 1.3 copy.56
  163.6 23.8 %collective-permute-done.2 = bf16[2,512,512]{1,2,0:T(8,128)(2,1)} collective-permute-done((bf16[2,512,512]{1,2,0:T(8,128)(2,1)S(1)}, bf16[2,512,512]{1,2,0:T(8,128)(2,1)}, u32[]{:S(2)}, u32[]{:S(2)}) %collective-permute-start.2) | collective-permute-done | bytes 1048608 | tf_op jit(solution)/shard_map/ppermute | solution.py:10
  187.4 1.3 select_bitcast_fusion.1
  188.7 1.3 copy.57
  190.0 18.8 %collective-permute-done.5 = bf16[2,512,512]{1,2,0:T(8,128)(2,1)} collective-permute-done((bf16[2,512,512]{1,2,0:T(8,128)(2,1)}, bf16[2,512,512]{1,2,0:T(8,128)(2,1)}, u32[]{:S(2)}, u32[]{:S(2)}) %collective-permute-start.5) | collective-permute-done | bytes 1048608 | tf_op jit(solution)/shard_map/ppermute | solution.py:10
  208.9 1.3 select_bitcast_fusion
  210.2 1.3 copy.58
  211.5 5.0 %fusion.18 = bf16[1,1,2,512,512]{4,2,3,1,0:T(2,128)(2,1)S(1)} fusion(bf16[8,512,512]{2,1,0:T(8,128)(2,1)} %all-gather.6.cloned.1.call-done, s32[2]{0:T(128)S(1)} %dynamic-slice_reduce_fusion), kind=kOutput, calls=%fused_computation.22 | convolution fusion | flops 8912912 | bytes 5242888 | tf_op jit(solution)/shard_map/kj,jab->kab/dot_general | solution.py:84
  216.5 1.1 copy.59
  (42 shorter events, 3.6 us)
Async XLA Ops:
  7.2 4.0 %copy-start.3 = (bf16[1,1,2,512,512]{4,3,2,1,0:T(8,128)(2,1)S(1)}, bf16[1,1,2,512,512]{4,3,2,1,0:T(8,128)(2,1)}, u32[]{:S(2)}) copy-start(bf16[1,1,2,512,512]{4,3,2,1,0:T(8,128)(2,1)} %param.13) | copy-start | bytes 3145732
  7.2 58.1 %all-gather.4.cloned.1.call-start = ((), (), s32[]{:S(2)}) async-start(), calls=%async_computation | async-start | bytes 5242880 | tf_op jit(solution)/shard_map/all_gather | solution.py:61
  7.9 203.6 %all-gather.6.cloned.1.call-start = ((), (), s32[]{:S(2)}) async-start(), calls=%async_computation.1 | async-start | bytes 5242880 | tf_op jit(solution)/shard_map/all_gather | solution.py:77
  8.8 3.7 %copy-start.11 = (s32[1,1,2]{2,1,0:T(1,128)S(1)}, s32[1,1,2]{2,1,0:T(1,128)}, u32[]{:S(2)}) copy-start(s32[1,1,2]{2,1,0:T(1,128)} %param.14) | copy-start | bytes 28
  8.8 3.7 %copy-start.1 = (bf16[1,1,2,512,512]{4,3,2,1,0:T(8,128)(2,1)S(1)}, bf16[1,1,2,512,512]{4,3,2,1,0:T(8,128)(2,1)}, u32[]{:S(2)}) copy-start(bf16[1,1,2,512,512]{4,3,2,1,0:T(8,128)(2,1)} %param.12) | copy-start | bytes 3145732
  70.2 1.6 copy-start.6
  71.0 1.7 copy-start
  72.8 3.8 %copy-start.2 = (bf16[1,1,2,512,512]{4,3,2,1,0:T(8,128)(2,1)S(1)}, bf16[1,1,2,512,512]{4,3,2,1,0:T(8,128)(2,1)}, u32[]{:S(2)}) copy-start(bf16[1,1,2,512,512]{4,3,2,1,0:T(8,128)(2,1)} %param.12) | copy-start | bytes 3145732
  72.8 3.8 %copy-start.9 = (bf16[1,1,2,512,512]{3,4,2,1,0:T(8,128)(2,1)S(1)}, bf16[1,1,2,512,512]{3,4,2,1,0:T(8,128)(2,1)}, u32[]{:S(2)}) copy-start(bf16[1,1,2,512,512]{3,4,2,1,0:T(8,128)(2,1)} %copy.35) | copy-start | bytes 3145732
  76.6 3.0 %copy-start.7 = (f32[1,1,2,512,512]{4,3,2,1,0:T(8,128)S(1)}, f32[1,1,2,512,512]{4,3,2,1,0:T(8,128)}, u32[]{:S(2)}) copy-start(f32[1,1,2,512,512]{4,3,2,1,0:T(8,128)} %param.11) | copy-start | bytes 6291460
  79.6 3.6 %copy-start.4 = (bf16[1,1,2,512,512]{4,3,2,1,0:T(8,128)(2,1)S(1)}, bf16[1,1,2,512,512]{4,3,2,1,0:T(8,128)(2,1)}, u32[]{:S(2)}) copy-start(bf16[1,1,2,512,512]{4,3,2,1,0:T(8,128)(2,1)} %param.13) | copy-start | bytes 3145732
  79.6 3.7 %copy-start.8 = (bf16[1,1,2,512,512]{3,4,2,1,0:T(8,128)(2,1)S(1)}, bf16[1,1,2,512,512]{3,4,2,1,0:T(8,128)(2,1)}, u32[]{:S(2)}) copy-start(bf16[1,1,2,512,512]{3,4,2,1,0:T(8,128)(2,1)} %copy.44) | copy-start | bytes 3145732
  83.3 2.1 copy-start.5
  87.7 2.7 %collective-permute-start = (bf16[2,512,512]{1,2,0:T(8,128)(2,1)S(1)}, bf16[2,512,512]{1,2,0:T(8,128)(2,1)S(1)}, u32[]{:S(2)}, u32[]{:S(2)}) collective-permute-start(bf16[2,512,512]{1,2,0:T(8,128)(2,1)S(1)} %copy-done.5), channel_id=1, source_target_pairs={{0,1},{1,0},{2,3},{3,2},{4,5},{5,4},{6,7},{7,6},{8,9},{9,8},{10,11... | collective-permute-start | bytes 3145736 | tf_op jit(solution)/shard_map/ppermute | solution.py:10
  87.8 4.3 %collective-permute-start.3 = (bf16[2,512,512]{1,2,0:T(8,128)(2,1)S(1)}, bf16[2,512,512]{1,2,0:T(8,128)(2,1)S(1)}, u32[]{:S(2)}, u32[]{:S(2)}) collective-permute-start(bf16[2,512,512]{1,2,0:T(8,128)(2,1)S(1)} %fusion.9), channel_id=1, source_target_pairs={{0,1},{1,0},{2,3},{3,2},{4,5},{5,4},{6,7},{7,6},{8,9},{9,8},{10,11... | collective-permute-start | bytes 3145736 | tf_op jit(solution)/shard_map/ppermute | solution.py:10
  90.6 26.1 %collective-permute-start.1 = (bf16[2,512,512]{1,2,0:T(8,128)(2,1)S(1)}, bf16[2,512,512]{1,2,0:T(8,128)(2,1)S(1)}, u32[]{:S(2)}, u32[]{:S(2)}) collective-permute-start(bf16[2,512,512]{1,2,0:T(8,128)(2,1)S(1)} %broadcast_select_fusion.1), channel_id=1, source_target_pairs={{0,2},{1,3},{2,0},{3,1},{4,6},{5,7},{6,4},{7,5},{8,10},{9,11},{10,... | collective-permute-start | bytes 3145736 | tf_op jit(solution)/shard_map/ppermute | solution.py:10
  92.3 67.4 %collective-permute-start.4 = (bf16[2,512,512]{1,2,0:T(8,128)(2,1)S(1)}, bf16[2,512,512]{1,2,0:T(8,128)(2,1)S(1)}, u32[]{:S(2)}, u32[]{:S(2)}) collective-permute-start(bf16[2,512,512]{1,2,0:T(8,128)(2,1)S(1)} %broadcast_select_fusion), channel_id=1, source_target_pairs={{0,2},{1,3},{2,0},{3,1},{4,6},{5,7},{6,4},{7,5},{8,10},{9,11},{10,... | collective-permute-start | bytes 3145736 | tf_op jit(solution)/shard_map/ppermute | solution.py:10
  116.7 44.0 %copy-start.10 = (s32[4,1,2]{0,2,1:T(2,128)S(1)}, s32[4,1,2]{0,2,1:T(2,128)}, u32[]{:S(2)}) copy-start(s32[4,1,2]{0,2,1:T(2,128)} %param.9) | copy-start | bytes 100
  116.8 70.6 %collective-permute-start.2 = (bf16[2,512,512]{1,2,0:T(8,128)(2,1)S(1)}, bf16[2,512,512]{1,2,0:T(8,128)(2,1)}, u32[]{:S(2)}, u32[]{:S(2)}) collective-permute-start(bf16[2,512,512]{1,2,0:T(8,128)(2,1)S(1)} %broadcast_select_fusion.3), channel_id=1, source_target_pairs={{0,4},{1,5},{2,6},{3,7},{4,0},{5,1},{6,2},{7,3},{8,12},{9,13},{10,... | collective-permute-start | bytes 3145736 | tf_op jit(solution)/shard_map/ppermute | solution.py:10
  160.8 48.1 %collective-permute-start.5 = (bf16[2,512,512]{1,2,0:T(8,128)(2,1)}, bf16[2,512,512]{1,2,0:T(8,128)(2,1)}, u32[]{:S(2)}, u32[]{:S(2)}) collective-permute-start(bf16[2,512,512]{1,2,0:T(8,128)(2,1)} %broadcast_select_fusion.2), channel_id=1, source_target_pairs={{0,4},{1,5},{2,6},{3,7},{4,0},{5,1},{6,2},{7,3},{8,12},{9,13},{10,... | collective-permute-start | bytes 3145736 | tf_op jit(solution)/shard_map/ppermute | solution.py:10
Sparse Core Ops, SparseCore 0:
  9.9 55.3 all-gather.3
  87.8 52.6 all-gather.5
where the time goes:
time: 225 us; the launch traced here: 224 us
  waiting for transfers between devices  151 us (67%)
  matrix products  36 us (16%)
  between operations  14.9 us (7%)
  local copies, waits for them, and re-layouts  12.2 us (5%)
  starting transfers between devices  6.02 us (3%)
  other arithmetic  4.17 us (2%)
    ppermute x6, waiting for transfers between devices, partner(): return lax.ppermute(value, axis, pairs)  108 us
    all_gather x1, waiting for transfers between devices, per_device(): lax.all_gather(grads, 'fsdp', axis=0, tiled=True)  42.9 us
    dot_general x8, matrix products, batched(): jnp.einsum('kab,kbc->kac', left, right, precision=lax.Precision.HIGHEST)  22.3 us
    unnamed x32, local copies, waits for them, and re-layouts  11.9 us
    ppermute x6, starting transfers between devices, partner(): return lax.ppermute(value, axis, pairs)  5.95 us
    dot_general x1, matrix products, per_device(): jnp.einsum('kj,jab->kab', home_pick, collected, preferred_element_type=jn...  4.98 us
    dot_general x1, matrix products, per_device(): jnp.einsum('sj,jab->sab', pick, everyone, preferred_element_type=jnp.floa...  4.95 us
  transfers between devices with their start and end apart: 8, of which 6 were waited for; matrix products, arithmetic and copies ran while one was open for 11% of the time, Pallas kernels for 0%

commit v1 on v0

v1 whole, which is shorter than its diff:
```python
import functools

import jax
import jax.numpy as jnp
from jax import lax
from jax.experimental import pallas as pl
from jax.experimental.pallas import tpu as pltpu
from jax.sharding import PartitionSpec as P

MESH = pl.DeviceIdType.MESH
CUTS = 4
AHEAD = 2


def flip(index, mask):
    bit = 1
    while bit <= mask:
        if mask & bit:
            index = index + bit - 2 * bit * ((index // bit) % 2)
        bit *= 2
    return index


def mm(left, right):
    return jnp.dot(left, right, preferred_element_type=jnp.float32)


def split(value):
    high = value.astype(jnp.bfloat16)
    low = (value - high.astype(jnp.float32)).astype(jnp.bfloat16)
    return high, low


def mm3(left, right):
    (lh, ll), (rh, rl) = left, right
    return mm(lh, rh) + (mm(lh, rl) + mm(ll, rh))


def kernel(
    groups,
    replicas,
    targets,
    refresh,
    offset,
    grads,
    lfac_hbm,
    rfac_hbm,
    lroot_hbm,
    rroot_hbm,
    nleft_hbm,
    nright_hbm,
    bleft_hbm,
    bright_hbm,
    precond_hbm,
    fac,
    root,
    fifth_hi,
    fifth_lo,
    send_g,
    recv_g,
    owned,
    fresh,
    result,
    send_r,
    recv_r,
    home,
    moved,
    in_sem,
    out_sem,
    buddy_out_sem,
    g_send,
    g_recv,
    r_send,
    r_recv,
    b_send,
    b_recv,
):
    per, width = grads.shape[0], grads.shape[1]
    me = lax.axis_index("fsdp")
    rep = lax.axis_index("rep")
    levels = replicas.bit_length() - 1
    rows = width // CUTS
    chunks = 2 * per * CUTS

    loads = []
    for s in range(per):
        for side, (f_hbm, x_hbm) in enumerate(((lfac_hbm, lroot_hbm), (rfac_hbm, rroot_hbm))):
            m = 2 * s + side
            loads.append(pltpu.make_async_copy(x_hbm.at[s], root.at[m], in_sem.at[0, m]))
            loads.append(pltpu.make_async_copy(f_hbm.at[s], fac.at[m], in_sem.at[1, m]))
    for load in loads:
        load.start()

    barrier = pltpu.get_barrier_semaphore()
    for j in range(1, groups):
        pl.semaphore_signal(barrier, inc=1, device_id=(flip(me, j), rep), device_id_type=MESH)
    for level in range(levels):
        pl.semaphore_signal(
            barrier, inc=1, device_id=(me, flip(rep, 1 << level)), device_id_type=MESH
        )

    def block_for(owner):
        index = jnp.int32(0)
        for k in range(1, per):
            index = jnp.where(targets[me, 0, k] // per == owner, k, index)
        return index

    order = sorted(range(1, groups), key=lambda j: -bin(j).count("1"))
    for j in order:
        send_g[j] = grads[block_for(flip(me, j))]
    pl.semaphore_wait(barrier, groups - 1 + levels)

    def exchange(source, target, send_sem, recv_sem, j):
        return pltpu.make_async_remote_copy(
            src_ref=source.at[j],
            dst_ref=target.at[j],
            send_sem=send_sem.at[j],
            recv_sem=recv_sem.at[j],
            device_id=(flip(me, j), rep),
            device_id_type=MESH,
        )

    outward = [exchange(send_g, recv_g, g_send, g_recv, j) for j in order]
    for copy in outward:
        copy.start()
    recv_g[0] = grads[block_for(me)]
    for load in loads:
        load.wait()

    def powers(m, carry):
        x = root[m]
        square = split(mm(x, x))
        fourth = split(mm3(square, square))
        hi, lo = split(mm(x, fourth[0]) + mm(x, fourth[1]))
        fifth_hi[m] = hi
        fifth_lo[m] = lo
        return carry

    lax.fori_loop(0, 2 * per, powers, 0)
    for copy in outward:
        copy.wait_recv()

    for s in range(per):
        place = jnp.int32(0)
        for j in range(1, groups):
            source = flip(me, j)
            for k in range(per):
                place = jnp.where(targets[source, 0, k] == me * per + s, j, place)
        owned[s] = recv_g[place]

    def buddy_copy(level_no, c):
        level = levels - 1 - level_no
        source = fresh if level_no == 0 else moved.at[level_no - 1]
        m, cut = c // CUTS, pl.multiple_of((c % CUTS) * rows, rows)
        return pltpu.make_async_remote_copy(
            src_ref=source.at[m, pl.ds(cut, rows)],
            dst_ref=moved.at[level_no, m, pl.ds(cut, rows)],
            send_sem=b_send.at[level_no, c],
            recv_sem=b_recv.at[level_no, c],
            device_id=(me, flip(rep, 1 << level)),
            device_id_type=MESH,
        )

    def newton(m, s, gram):
        factor = split(fac[m] + gram)
        moment = mm3((fifth_hi[m], fifth_lo[m]), factor)
        old = root[m].astype(jnp.float32)
        new = (5.0 * old - moment) / 4.0
        fresh[m] = jnp.where(refresh[0, 0, s] == 1, new, old).astype(jnp.bfloat16)

    stores = []
    for s in range(per):
        block = owned[s]
        newton(
            2 * s,
            s,
            lax.dot_general(block, block, (((1,), (1,)), ((), ())), preferred_element_type=jnp.float32),
        )
        if s == 0:
            for c in range(AHEAD):
                buddy_copy(0, c).start()
        newton(
            2 * s + 1,
            s,
            lax.dot_general(block, block, (((0,), (0,)), ((), ())), preferred_element_type=jnp.float32),
        )
        half = mm(fresh[2 * s], block).astype(jnp.bfloat16)
        result[s] = mm(half, fresh[2 * s + 1]).astype(jnp.bfloat16)
        for side, out in enumerate((nleft_hbm, nright_hbm)):
            m = 2 * s + side
            stores.append(pltpu.make_async_copy(fresh.at[m], out.at[s], out_sem.at[m]))
            stores[-1].start()

    for j in [0] + order:
        index = jnp.int32(0)
        for k in range(per):
            there = targets[flip(me, j), 0, k]
            index = jnp.where(there // per == me, there % per, index)
        if j == 0:
            recv_r[0] = result[index]
        else:
            send_r[j] = result[index]
    backward = [exchange(send_r, recv_r, r_send, r_recv, j) for j in order]
    for copy in backward:
        copy.start()

    def buddy_store(c, wait):
        s, cut = c // (2 * CUTS), pl.multiple_of((c % CUTS) * rows, rows)
        for side, out in enumerate((bleft_hbm, bright_hbm)):

            @pl.when((c // CUTS) % 2 == side)
            def _():
                copy = pltpu.make_async_copy(
                    moved.at[levels - 1, 2 * s + side, pl.ds(cut, rows)],
                    out.at[s, pl.ds(cut, rows)],
                    buddy_out_sem.at[c],
                )
                if wait:
                    copy.wait()
                else:
                    copy.start()

    def step(t, carry):
        @pl.when(t < chunks)
        def _():
            buddy_copy(0, t).start()

        for n in range(levels):
            c = t - AHEAD - n

            @pl.when(jnp.logical_and(c >= 0, c < chunks))
            def _():
                buddy_copy(n, c).wait_recv()
                m, cut = c // CUTS, pl.multiple_of((c % CUTS) * rows, rows)
                level = levels - 1 - n
                crossing = (offset[0] // (1 << level)) % 2 == 1
                here = fresh if n == 0 else moved.at[n - 1]
                mine = here[m, pl.ds(cut, rows)].astype(jnp.float32)
                theirs = moved[n, m, pl.ds(cut, rows)].astype(jnp.float32)
                moved[n, m, pl.ds(cut, rows)] = jnp.where(crossing, theirs, mine).astype(
                    jnp.bfloat16
                )
                if n < levels - 1:
                    buddy_copy(n + 1, c).start()
                else:
                    buddy_store(c, False)

        return carry

    lax.fori_loop(AHEAD, chunks, step, 0)

    for copy in backward:
        copy.wait_recv()
    for k in range(per):
        place = jnp.int32(0)
        for j in range(1, groups):
            place = jnp.where(targets[me, 0, k] // per == flip(me, j), j, place)
        home[k] = recv_r[place]
    stores.append(pltpu.make_async_copy(home, precond_hbm, out_sem.at[2 * per]))
    stores[-1].start()

    lax.fori_loop(chunks, chunks + AHEAD + levels - 1, step, 0)

    for copy in stores:
        copy.wait()
    for copy in outward + backward:
        copy.wait_send()

    def drain(c, carry):
        for n in range(levels):
            buddy_copy(n, c).wait_send()
        buddy_store(c, True)
        return carry

    lax.fori_loop(0, chunks, drain, 0)


def per_device(
    groups,
    replicas,
    grads,
    targets,
    left_factor,
    right_factor,
    left_root,
    right_root,
    refresh,
    buddy_offset,
):
    per, width = grads.shape[2], grads.shape[3]
    levels = replicas.bit_length() - 1
    chunks = 2 * per * CUTS
    shape = grads.shape
    blocks = (per, width, width)
    bf = jnp.bfloat16
    smem = pl.BlockSpec(memory_space=pltpu.SMEM)
    vmem = pl.BlockSpec(memory_space=pltpu.VMEM)
    hbm = pl.BlockSpec(memory_space=pl.ANY)
    dma = pltpu.SemaphoreType.DMA
    matrices = (2 * per, width, width)
    slots = (groups, width, width)
    products = 2 * per * 10 + 2 * per
    outs = pl.pallas_call(
        functools.partial(kernel, groups, replicas),
        out_shape=[jax.ShapeDtypeStruct(blocks, bf)] * 5,
        in_specs=[smem, smem, smem, vmem, hbm, hbm, hbm, hbm],
        out_specs=[hbm] * 5,
        scratch_shapes=[
            pltpu.VMEM(matrices, jnp.float32),
            pltpu.VMEM(matrices, bf),
            pltpu.VMEM(matrices, bf),
            pltpu.VMEM(matrices, bf),
            pltpu.VMEM(slots, bf),
            pltpu.VMEM(slots, bf),
            pltpu.VMEM(blocks, bf),
            pltpu.VMEM(matrices, bf),
            pltpu.VMEM(blocks, bf),
            pltpu.VMEM(slots, bf),
            pltpu.VMEM(slots, bf),
            pltpu.VMEM(blocks, bf),
            pltpu.VMEM((levels,) + matrices, bf),
            dma((2, 2 * per)),
            dma((2 * per + 1,)),
            dma((chunks,)),
            dma((groups,)),
            dma((groups,)),
            dma((groups,)),
            dma((groups,)),
            dma((levels, chunks)),
            dma((levels, chunks)),
        ],
        compiler_params=pltpu.CompilerParams(
            collective_id=0, has_side_effects=True, vmem_limit_bytes=56 * 1024 * 1024
        ),
        cost_estimate=pl.CostEstimate(
            flops=products * 2 * width**3, bytes_accessed=24 * per * width**2, transcendentals=0
        ),
        name="refresh_and_exchange",
    )(
        targets,
        refresh,
        buddy_offset,
        grads.reshape(blocks),
        left_factor.reshape(blocks),
        right_factor.reshape(blocks),
        left_root.reshape(blocks),
        right_root.reshape(blocks),
    )
    return tuple(out.reshape(shape) for out in outs)


def solution(mesh):
    blocks = P("fsdp", "rep", None, None, None)
    placed = (
        blocks,
        P(None, "rep", None),
        blocks,
        blocks,
        blocks,
        blocks,
        P("fsdp", "rep", None),
        P("fsdp"),
    )
    return jax.shard_map(
        functools.partial(per_device, mesh.shape["fsdp"], mesh.shape["rep"]),
        mesh=mesh,
        in_specs=placed,
        out_specs=(blocks,) * 5,
        check_vma=False,
    )
```

time: 225 us -> 140 us (0.62)
  waiting for transfers between devices: 151 us -> 0 us
  Pallas kernels: 0 us -> 129 us
  matrix products: 36 us -> 0 us
  between operations: 14.9 us -> 1.31 us
  starting transfers between devices: 6.02 us -> 0 us
  local copies, waits for them, and re-layouts: 12.2 us -> 7.64 us
  other arithmetic: 4.17 us -> 0 us
    pallas_call x0 -> x1, Pallas kernels: none -> 129 us  [per_device(): pl.pallas_call(functools.partial(kernel, groups, replicas), out_shape=[ja...]
    ppermute x6 -> x0, waiting for transfers between devices: 108 us -> none  [partner(): return lax.ppermute(value, axis, pairs)]
    all_gather x2 -> x0, waiting for transfers between devices: 42.9 us -> none  [the longest x1 42.9 us: per_device(): lax.all_gather(grads, 'fsdp', axis=0, tiled=True)]
    dot_general x13 -> x0, matrix products: 36 us -> none  [the longest x8 22.3 us: batched(): jnp.einsum('kab,kbc->kac', left, right, precision=lax.Precision.HIGHEST)]
    ppermute x6 -> x0, starting transfers between devices: 5.95 us -> none  [partner(): return lax.ppermute(value, axis, pairs)]
    unnamed x32 -> x14, local copies, waits for them, and re-layouts: 11.9 us -> 7.64 us
    reshape x2 -> x0, other arithmetic: 2.67 us -> none  [the longest x1 1.34 us: per_device(): copies[1].reshape(shape)]
  transfers between devices with their start and end apart: 8 -> 0, of which waited for: 6 -> 0; matrix products, arithmetic and copies ran while one was open for 11% -> 0% of each run, Pallas kernels for 0% -> 0%
where the time goes in v1:
time: 140 us; the launch traced here: 138 us
  Pallas kernels  129 us (92%)
  local copies, waits for them, and re-layouts  7.64 us (5%)
    pallas_call x1, Pallas kernels, per_device(): pl.pallas_call(functools.partial(kernel, groups, replicas), out_shape=[ja...  129 us
    unnamed x14, local copies, waits for them, and re-layouts  7.64 us

profile of v1, /device:TPU:0, one launch (start us, length us, event | category | flops | bytes accessed | tf_op | source)
XLA Modules:
  0.0 138.4 jit_solution(13114737159318482412)
XLA Ops:
  1.3 1.3 copy.13.targets
  2.6 129.4 %refresh_and_exchange.1 = (bf16[2,512,512]{2,1,0:T(8,128)(2,1)}, bf16[2,512,512]{2,1,0:T(8,128)(2,1)}, bf16[2,512,512]{2,1,0:T(8,128)(2,1)}, bf16[2,512,512]{2,1,0:T(8,128)(2,1)}, bf16[2,512,512]{2,1,0:T(8,128)(2,1)}) custom-call(s32[4,1,2]{2,1,0:T(1,128)} %copy.13.targets, s32[1,1,2]{2,1,0:T(1,128)} %refresh.1, s32[1]{0:T(128)S(6)} %copy.19.offset, ...), custom_call_target="tpu_custom_call" | custom-call | flops 11811160064 | bytes 12582912 | tf_op jit(solution)/shard_map/refresh_and_exchange/pallas_call | solution.py:303
  132.1 0.0 copy-start.3
  132.1 0.0 copy-start.2
  132.1 2.4 %copy.20 = bf16[1,1,2,512,512]{4,3,2,1,0:T(8,128)(2,1)} copy(bf16[1,1,2,512,512]{4,3,2,1,0:T(8,128)(2,1)} %bitcast.14) | data formatting | bytes 2097152
  134.5 0.0 copy-done.3
  134.5 0.0 copy-start.1
  134.5 1.0 copy.21
  135.5 0.0 copy-done.2
  135.5 0.0 copy-start
  135.5 1.0 copy.22
  136.4 0.0 copy-done.1
  136.4 1.0 copy.23
  137.4 0.0 copy-done
  137.4 1.0 copy.24
Async XLA Ops:
  132.1 2.4 %copy-start.3 = (bf16[2,512,512]{2,1,0:T(8,128)(2,1)S(1)}, bf16[2,512,512]{2,1,0:T(8,128)(2,1)}, u32[]{:S(2)}) copy-start(bf16[2,512,512]{2,1,0:T(8,128)(2,1)} %get-tuple-element.11) | copy-start | bytes 3145732
  132.1 3.4 %copy-start.2 = (bf16[2,512,512]{2,1,0:T(8,128)(2,1)S(1)}, bf16[2,512,512]{2,1,0:T(8,128)(2,1)}, u32[]{:S(2)}) copy-start(bf16[2,512,512]{2,1,0:T(8,128)(2,1)} %get-tuple-element.12) | copy-start | bytes 3145732
  134.5 1.9 %copy-start.1 = (bf16[2,512,512]{2,1,0:T(8,128)(2,1)S(1)}, bf16[2,512,512]{2,1,0:T(8,128)(2,1)}, u32[]{:S(2)}) copy-start(bf16[2,512,512]{2,1,0:T(8,128)(2,1)} %get-tuple-element.13) | copy-start | bytes 3145732
  135.5 1.9 %copy-start = (bf16[2,512,512]{2,1,0:T(8,128)(2,1)S(1)}, bf16[2,512,512]{2,1,0:T(8,128)(2,1)}, u32[]{:S(2)}) copy-start(bf16[2,512,512]{2,1,0:T(8,128)(2,1)} %get-tuple-element.14) | copy-start | bytes 3145732

commit v2 on v1

--- a/solution.py
+++ b/solution.py
@@ -8,8 +8,8 @@
 from jax.sharding import PartitionSpec as P
 
 MESH = pl.DeviceIdType.MESH
-CUTS = 4
-AHEAD = 2
+CUTS = 8
+AHEAD = 3
 
 
 def flip(index, mask):
@@ -102,7 +102,7 @@
     def block_for(owner):
         index = jnp.int32(0)
         for k in range(1, per):
-            index = jnp.where(targets[me, 0, k] // per == owner, k, index)
+            index = jnp.where(targets[k, me] // per == owner, k, index)
         return index
 
     order = sorted(range(1, groups), key=lambda j: -bin(j).count("1"))
@@ -145,7 +145,7 @@
         for j in range(1, groups):
             source = flip(me, j)
             for k in range(per):
-                place = jnp.where(targets[source, 0, k] == me * per + s, j, place)
+                place = jnp.where(targets[k, source] == me * per + s, j, place)
         owned[s] = recv_g[place]
 
     def buddy_copy(level_no, c):
@@ -166,7 +166,7 @@
         moment = mm3((fifth_hi[m], fifth_lo[m]), factor)
         old = root[m].astype(jnp.float32)
         new = (5.0 * old - moment) / 4.0
-        fresh[m] = jnp.where(refresh[0, 0, s] == 1, new, old).astype(jnp.bfloat16)
+        fresh[m] = jnp.where(refresh[s] == 1, new, old).astype(jnp.bfloat16)
 
     stores = []
     for s in range(per):
@@ -194,7 +194,7 @@
     for j in [0] + order:
         index = jnp.int32(0)
         for k in range(per):
-            there = targets[flip(me, j), 0, k]
+            there = targets[k, flip(me, j)]
             index = jnp.where(there // per == me, there % per, index)
         if j == 0:
             recv_r[0] = result[index]
@@ -254,7 +254,7 @@
     for k in range(per):
         place = jnp.int32(0)
         for j in range(1, groups):
-            place = jnp.where(targets[me, 0, k] // per == flip(me, j), j, place)
+            place = jnp.where(targets[k, me] // per == flip(me, j), j, place)
         home[k] = recv_r[place]
     stores.append(pltpu.make_async_copy(home, precond_hbm, out_sem.at[2 * per]))
     stores[-1].start()
@@ -273,6 +273,21 @@
         return carry
 
     lax.fori_loop(0, chunks, drain, 0)
+
+
+def hand_on(*refs):
+    sources, targets, sem = refs[:5], refs[5:10], refs[10]
+    copies = []
+    for i in range(5):
+        for half in range(2):
+            part = pl.ds(half, 1) if sources[i].shape[0] == 2 else pl.ds(0, sources[i].shape[0])
+            copies.append(
+                pltpu.make_async_copy(sources[i].at[part], targets[i].at[part], sem.at[i, half])
+            )
+    for copy in copies:
+        copy.start()
+    for copy in copies:
+        copy.wait()
 
 
 def per_device(
@@ -337,8 +352,8 @@
         ),
         name="refresh_and_exchange",
     )(
-        targets,
-        refresh,
+        targets.transpose(1, 2, 0).reshape(per, groups),
+        refresh.reshape(per),
         buddy_offset,
         grads.reshape(blocks),
         left_factor.reshape(blocks),
@@ -346,6 +361,14 @@
         left_root.reshape(blocks),
         right_root.reshape(blocks),
     )
+    outs = pl.pallas_call(
+        hand_on,
+        out_shape=[jax.ShapeDtypeStruct(blocks, bf)] * 5,
+        in_specs=[hbm] * 5,
+        out_specs=[hbm] * 5,
+        scratch_shapes=[dma((5, 2))],
+        name="hand_on",
+    )(*outs)
     return tuple(out.reshape(shape) for out in outs)
 
 

time: 140 us -> 293 us (2.09)
  Pallas kernels: 129 us -> 290 us
  local copies, waits for them, and re-layouts: 7.64 us -> 0 us
    pallas_call x0 -> x1, Pallas kernels: none -> 160 us  [per_device(): pl.pallas_call(hand_on, out_shape=[jax.ShapeDtypeStruct(blocks, bf)] * 5,...]
    unnamed x14 -> x0, local copies, waits for them, and re-layouts: 7.64 us -> none
where the time goes in v2:
time: 293 us; the launch traced here: 291 us
  Pallas kernels  290 us (99%)
    pallas_call x1, Pallas kernels, per_device(): pl.pallas_call(hand_on, out_shape=[jax.ShapeDtypeStruct(blocks, bf)] * 5,...  160 us
    pallas_call x1, Pallas kernels, per_device(): pl.pallas_call(functools.partial(kernel, groups, replicas), out_shape=[ja...  130 us

profile of v2, /device:TPU:0, one launch (start us, length us, event | category | flops | bytes accessed | tf_op | source)
XLA Modules:
  0.0 291.2 jit_solution(3058086443127584431)
XLA Ops:
  1.3 129.9 %refresh_and_exchange.1 = (bf16[2,512,512]{2,1,0:T(8,128)(2,1)}, bf16[2,512,512]{2,1,0:T(8,128)(2,1)}, bf16[2,512,512]{2,1,0:T(8,128)(2,1)}, bf16[2,512,512]{2,1,0:T(8,128)(2,1)}, bf16[2,512,512]{2,1,0:T(8,128)(2,1)}) custom-call(s32[2,4]{1,0:T(2,128)} %bitcast.24, s32[2]{0:T(128)} %bitcast.25, s32[1]{0:T(128)S(6)} %copy.13.offset, ...), custom_call_target="tpu_custom_call" | custom-call | flops 11811160064 | bytes 12582912 | tf_op jit(solution)/shard_map/refresh_and_exchange/pallas_call | solution.py:318
  131.1 160.0 %hand_on.1 = (bf16[2,512,512]{2,1,0:T(8,128)(2,1)}, bf16[2,512,512]{2,1,0:T(8,128)(2,1)}, bf16[2,512,512]{2,1,0:T(8,128)(2,1)}, bf16[2,512,512]{2,1,0:T(8,128)(2,1)}, bf16[2,512,512]{2,1,0:T(8,128)(2,1)}) custom-call(bf16[2,512,512]{2,1,0:T(8,128)(2,1)} %get-tuple-element.15.refs_0_, bf16[2,512,512]{2,1,0:T(8,128)(2,1)} %get-tuple-element.16.refs_1_, ...), custom_call_target="tpu_custom_call" | custom-call | tf_op jit(solution)/shard_map/hand_on/pallas_call | solution.py:364

commit v3 on v2

--- a/solution.py
+++ b/solution.py
@@ -9,7 +9,8 @@
 
 MESH = pl.DeviceIdType.MESH
 CUTS = 8
-AHEAD = 3
+AHEAD = 4
+BEHIND = 3
 
 
 def flip(index, mask):
@@ -226,7 +227,7 @@
             buddy_copy(0, t).start()
 
         for n in range(levels):
-            c = t - AHEAD - n
+            c = t - AHEAD - BEHIND * n
 
             @pl.when(jnp.logical_and(c >= 0, c < chunks))
             def _():
@@ -259,7 +260,7 @@
     stores.append(pltpu.make_async_copy(home, precond_hbm, out_sem.at[2 * per]))
     stores[-1].start()
 
-    lax.fori_loop(chunks, chunks + AHEAD + levels - 1, step, 0)
+    lax.fori_loop(chunks, chunks + AHEAD + BEHIND * (levels - 1), step, 0)
 
     for copy in stores:
         copy.wait()
@@ -276,18 +277,23 @@
 
 
 def hand_on(*refs):
-    sources, targets, sem = refs[:5], refs[5:10], refs[10]
-    copies = []
+    sources, targets, (stage, load_sem, store_sem) = refs[:5], refs[5:10], refs[10:]
+    loads, stores = [], []
     for i in range(5):
-        for half in range(2):
-            part = pl.ds(half, 1) if sources[i].shape[0] == 2 else pl.ds(0, sources[i].shape[0])
-            copies.append(
-                pltpu.make_async_copy(sources[i].at[part], targets[i].at[part], sem.at[i, half])
+        for s in range(sources[i].shape[0]):
+            loads.append(
+                pltpu.make_async_copy(sources[i].at[s], stage.at[i, s], load_sem.at[i, s])
             )
-    for copy in copies:
-        copy.start()
-    for copy in copies:
-        copy.wait()
+            stores.append(
+                pltpu.make_async_copy(stage.at[i, s], targets[i].at[s], store_sem.at[i, s])
+            )
+    for load in loads:
+        load.start()
+    for load, store in zip(loads, stores):
+        load.wait()
+        store.start()
+    for store in stores:
+        store.wait()
 
 
 def per_device(
@@ -366,7 +372,7 @@
         out_shape=[jax.ShapeDtypeStruct(blocks, bf)] * 5,
         in_specs=[hbm] * 5,
         out_specs=[hbm] * 5,
-        scratch_shapes=[dma((5, 2))],
+        scratch_shapes=[pltpu.VMEM((5,) + blocks, bf), dma((5, per)), dma((5, per))],
         name="hand_on",
     )(*outs)
     return tuple(out.reshape(shape) for out in outs)

time: 293 us -> 137 us (0.47)
  Pallas kernels: 290 us -> 134 us
    pallas_call x1, Pallas kernels: 160 us -> 4.71 us  [per_device(): pl.pallas_call(hand_on, out_shape=[jax.ShapeDtypeStruct(blocks, bf)] * 5,...]
where the time goes in v3:
time: 137 us; the launch traced here: 135 us
  Pallas kernels  134 us (98%)
    pallas_call x1, Pallas kernels, per_device(): pl.pallas_call(functools.partial(kernel, groups, replicas), out_shape=[ja...  129 us
    pallas_call x1, Pallas kernels, per_device(): pl.pallas_call(hand_on, out_shape=[jax.ShapeDtypeStruct(blocks, bf)] * 5,...  4.71 us

profile of v3, /device:TPU:0, one launch (start us, length us, event | category | flops | bytes accessed | tf_op | source)
XLA Modules:
  0.0 135.2 jit_solution(8833810746992394986)
XLA Ops:
  1.3 129.2 %refresh_and_exchange.1 = (bf16[2,512,512]{2,1,0:T(8,128)(2,1)}, bf16[2,512,512]{2,1,0:T(8,128)(2,1)}, bf16[2,512,512]{2,1,0:T(8,128)(2,1)}, bf16[2,512,512]{2,1,0:T(8,128)(2,1)}, bf16[2,512,512]{2,1,0:T(8,128)(2,1)}) custom-call(s32[2,4]{1,0:T(2,128)} %bitcast.24, s32[2]{0:T(128)} %bitcast.25, s32[1]{0:T(128)S(6)} %copy.13.offset, ...), custom_call_target="tpu_custom_call" | custom-call | flops 11811160064 | bytes 12582912 | tf_op jit(solution)/shard_map/refresh_and_exchange/pallas_call | solution.py:324
  130.4 4.7 %hand_on.1 = (bf16[2,512,512]{2,1,0:T(8,128)(2,1)}, bf16[2,512,512]{2,1,0:T(8,128)(2,1)}, bf16[2,512,512]{2,1,0:T(8,128)(2,1)}, bf16[2,512,512]{2,1,0:T(8,128)(2,1)}, bf16[2,512,512]{2,1,0:T(8,128)(2,1)}) custom-call(bf16[2,512,512]{2,1,0:T(8,128)(2,1)} %get-tuple-element.15.refs_0_, bf16[2,512,512]{2,1,0:T(8,128)(2,1)} %get-tuple-element.16.refs_1_, ...), custom_call_target="tpu_custom_call" | custom-call | tf_op jit(solution)/shard_map/hand_on/pallas_call | solution.py:370

commit v4 on v3

v4 whole, which is shorter than its diff:
```python
import functools

import jax
import jax.numpy as jnp
from jax import lax
from jax.experimental import pallas as pl
from jax.experimental.pallas import tpu as pltpu
from jax.sharding import PartitionSpec as P

MESH = pl.DeviceIdType.MESH
CUTS = 8
PARTS = 16
AHEAD = 4
BEHIND = 3


def flip(index, mask):
    bit = 1
    while bit <= mask:
        if mask & bit:
            index = index + bit - 2 * bit * ((index // bit) % 2)
        bit *= 2
    return index


def mm(left, right):
    return jnp.dot(left, right, preferred_element_type=jnp.float32)


def split(value):
    high = value.astype(jnp.bfloat16)
    low = (value - high.astype(jnp.float32)).astype(jnp.bfloat16)
    return high, low


def mm3(left, right):
    (lh, ll), (rh, rl) = left, right
    return mm(lh, rh) + (mm(lh, rl) + mm(ll, rh))


def refresh_kernel(
    groups,
    targets,
    refresh,
    offset,
    grads,
    lfac_hbm,
    rfac_hbm,
    lroot_hbm,
    rroot_hbm,
    fresh_hbm,
    result_hbm,
    offsets_out,
    fac,
    root,
    fifth_hi,
    fifth_lo,
    send_g,
    recv_g,
    owned,
    fresh,
    result,
    offsets,
    in_sem,
    out_sem,
    g_send,
    g_recv,
    o_send,
    o_recv,
):
    per, width = grads.shape[0], grads.shape[1]
    me = lax.axis_index("fsdp")
    rep = lax.axis_index("rep")

    loads = []
    for s in range(per):
        for side, (f_hbm, x_hbm) in enumerate(((lfac_hbm, lroot_hbm), (rfac_hbm, rroot_hbm))):
            m = side * per + s
            loads.append(pltpu.make_async_copy(x_hbm.at[s], root.at[m], in_sem.at[0, m]))
            loads.append(pltpu.make_async_copy(f_hbm.at[s], fac.at[m], in_sem.at[1, m]))
    for load in loads:
        load.start()

    barrier = pltpu.get_barrier_semaphore()
    for j in range(1, groups):
        pl.semaphore_signal(barrier, inc=1, device_id=(flip(me, j), rep), device_id_type=MESH)

    def block_for(owner):
        index = jnp.int32(0)
        for k in range(1, per):
            index = jnp.where(targets[k, me] // per == owner, k, index)
        return index

    order = sorted(range(1, groups), key=lambda j: -bin(j).count("1"))
    for j in order:
        send_g[j] = grads[block_for(flip(me, j))]
    offsets[0] = jnp.full(offsets.shape[1:], offset[0], jnp.int32)
    pl.semaphore_wait(barrier, groups - 1)

    def exchange(source, j, target, send_sem, recv_sem):
        return pltpu.make_async_remote_copy(
            src_ref=source,
            dst_ref=target.at[j],
            send_sem=send_sem.at[j],
            recv_sem=recv_sem.at[j],
            device_id=(flip(me, j), rep),
            device_id_type=MESH,
        )

    outward = [exchange(offsets.at[0], j, offsets, o_send, o_recv) for j in order]
    outward += [exchange(send_g.at[j], j, recv_g, g_send, g_recv) for j in order]
    for copy in outward:
        copy.start()
    recv_g[0] = grads[block_for(me)]
    for load in loads:
        load.wait()

    def powers(m, carry):
        x = root[m]
        square = split(mm(x, x))
        fourth = split(mm3(square, square))
        hi, lo = split(mm(x, fourth[0]) + mm(x, fourth[1]))
        fifth_hi[m] = hi
        fifth_lo[m] = lo
        return carry

    lax.fori_loop(0, 2 * per, powers, 0)
    for copy in outward:
        copy.wait_recv()

    for s in range(per):
        place = jnp.int32(0)
        for j in range(1, groups):
            source = flip(me, j)
            for k in range(per):
                place = jnp.where(targets[k, source] == me * per + s, j, place)
        owned[s] = recv_g[place]

    def newton(m, s, gram):
        factor = split(fac[m] + gram)
        moment = mm3((fifth_hi[m], fifth_lo[m]), factor)
        old = root[m].astype(jnp.float32)
        new = (5.0 * old - moment) / 4.0
        fresh[m] = jnp.where(refresh[s] == 1, new, old).astype(jnp.bfloat16)

    def gram(block, dim):
        dims = (((dim,), (dim,)), ((), ()))
        return lax.dot_general(block, block, dims, preferred_element_type=jnp.float32)

    stores = []
    for s in range(per):
        block = owned[s]
        newton(s, s, gram(block, 1))
        newton(per + s, s, gram(block, 0))
        for m in (s, per + s):
            stores.append(pltpu.make_async_copy(fresh.at[m], fresh_hbm.at[m], out_sem.at[m]))
            stores[-1].start()
        half = mm(fresh[s], block).astype(jnp.bfloat16)
        result[s] = mm(half, fresh[per + s]).astype(jnp.bfloat16)
        stores.append(
            pltpu.make_async_copy(result.at[s], result_hbm.at[s], out_sem.at[2 * per + s])
        )
        stores[-1].start()
    offsets_out[...] = offsets[...]
    for copy in stores:
        copy.wait()
    for copy in outward:
        copy.wait_send()


def greet(peers):
    barrier = pltpu.get_barrier_semaphore()
    for peer in peers:
        pl.semaphore_signal(barrier, inc=1, device_id=peer, device_id_type=MESH)
    pl.semaphore_wait(barrier, len(peers))


def choose(condition, one, other):
    return jnp.where(condition, one.astype(jnp.float32), other.astype(jnp.float32)).astype(
        jnp.bfloat16
    )


class Homeward:
    def __init__(self, groups, targets, result, send, recv, send_sem, recv_sem):
        self.groups, self.per, self.targets = groups, result.shape[0], targets
        self.recv = recv
        self.me, self.rep = lax.axis_index("fsdp"), lax.axis_index("rep")
        self.order = sorted(range(1, groups), key=lambda j: -bin(j).count("1"))
        for j in [0] + self.order:
            index = jnp.int32(0)
            for k in range(self.per):
                there = targets[k, flip(self.me, j)]
                index = jnp.where(there // self.per == self.me, there % self.per, index)
            (recv if j == 0 else send)[j] = result[index]
        self.copies = [
            pltpu.make_async_remote_copy(
                src_ref=send.at[j],
                dst_ref=recv.at[j],
                send_sem=send_sem.at[j],
                recv_sem=recv_sem.at[j],
                device_id=(flip(self.me, j), self.rep),
                device_id_type=MESH,
            )
            for j in self.order
        ]

    def start(self):
        for copy in self.copies:
            copy.start()

    def finish(self, home):
        for copy in self.copies:
            copy.wait_recv()
        for k in range(self.per):
            place = jnp.int32(0)
            for j in range(1, self.groups):
                owner = self.targets[k, self.me] // self.per
                place = jnp.where(owner == flip(self.me, j), j, place)
            home[k] = self.recv[place]

    def wait_send(self):
        for copy in self.copies:
            copy.wait_send()


def butterfly_kernel(
    groups,
    replicas,
    offsets,
    targets,
    fresh,
    result,
    buddy_hbm,
    precond_hbm,
    send_r,
    recv_r,
    home,
    moved,
    store_sem,
    home_sem,
    r_send,
    r_recv,
    b_send,
    b_recv,
):
    matrices, width = fresh.shape[0], fresh.shape[1]
    me, rep = lax.axis_index("fsdp"), lax.axis_index("rep")
    levels = replicas.bit_length() - 1
    rows = width // CUTS
    chunks = matrices * CUTS
    greet(
        [(flip(me, j), rep) for j in range(1, groups)]
        + [(me, flip(rep, 1 << level)) for level in range(levels)]
    )
    homeward = Homeward(groups, targets, result, send_r, recv_r, r_send, r_recv)
    homeward.start()

    def spot(c):
        return c // CUTS, pl.ds(pl.multiple_of((c % CUTS) * rows, rows), rows)

    def buddy_copy(n, c):
        source = fresh if n == 0 else moved.at[n - 1]
        m, part = spot(c)
        return pltpu.make_async_remote_copy(
            src_ref=source.at[m, part],
            dst_ref=moved.at[n, m, part],
            send_sem=b_send.at[n, c],
            recv_sem=b_recv.at[n, c],
            device_id=(me, flip(rep, 1 << (levels - 1 - n))),
            device_id_type=MESH,
        )

    def buddy_store(c):
        m, part = spot(c)
        return pltpu.make_async_copy(
            moved.at[levels - 1, m, part], buddy_hbm.at[m, part], store_sem.at[c]
        )

    def step(t, carry):
        @pl.when(t < chunks)
        def _():
            buddy_copy(0, t).start()

        for n in range(levels):
            c = t - AHEAD - BEHIND * n

            @pl.when(jnp.logical_and(c >= 0, c < chunks))
            def _():
                buddy_copy(n, c).wait_recv()
                m, part = spot(c)
                crossing = (offsets[0] // (1 << (levels - 1 - n))) % 2 == 1
                here = fresh if n == 0 else moved.at[n - 1]
                moved[n, m, part] = choose(crossing, moved[n, m, part], here[m, part])
                if n < levels - 1:
                    buddy_copy(n + 1, c).start()
                else:
                    buddy_store(c).start()

        return carry

    lax.fori_loop(0, chunks, step, 0)
    homeward.finish(home)
    bring = pltpu.make_async_copy(home, precond_hbm, home_sem.at[0])
    bring.start()
    lax.fori_loop(chunks, chunks + AHEAD + BEHIND * (levels - 1), step, 0)
    bring.wait()
    homeward.wait_send()

    def drain(c, carry):
        for n in range(levels):
            buddy_copy(n, c).wait_send()
        buddy_store(c).wait()
        return carry

    lax.fori_loop(0, chunks, drain, 0)


def spread_kernel(
    offsets,
    targets,
    fresh,
    result,
    buddy_hbm,
    precond_hbm,
    send_r,
    recv_r,
    home,
    twin,
    ready,
    guest,
    far_out,
    far_in,
    far,
    near_out,
    near_in,
    near,
    back,
    store_sem,
    home_sem,
    r_send,
    r_recv,
    t_send,
    t_recv,
    g_send,
    g_recv,
    f_send,
    f_recv,
    n_send,
    n_recv,
    b_send,
    b_recv,
):
    groups, width = fresh.shape[0], fresh.shape[1]
    me, rep = lax.axis_index("fsdp"), lax.axis_index("rep")
    others = range(1, groups)
    rows = width // PARTS
    greet(
        [(flip(me, j), rep) for j in others] + [(me, flip(rep, 1 << level)) for level in range(3)]
    )

    def span(c):
        return pl.ds(pl.multiple_of(c * rows, rows), rows)

    def send(source, target, send_sem, recv_sem, device):
        return pltpu.make_async_remote_copy(
            src_ref=source,
            dst_ref=target,
            send_sem=send_sem,
            recv_sem=recv_sem,
            device_id=device,
            device_id_type=MESH,
        )

    def to_twin(c):
        part = (slice(None), span(c))
        return send(
            fresh.at[part], twin.at[part], t_send.at[c], t_recv.at[c], (me, flip(rep, 1))
        )

    def to_guest(j, c):
        part = (j, span(c))
        return send(
            ready.at[part], guest.at[part], g_send.at[j, c], g_recv.at[j, c], (flip(me, j), rep)
        )

    def to_far(c):
        part = (slice(None), span(c))
        return send(
            far_out.at[part], far_in.at[part], f_send.at[c], f_recv.at[c], (me, flip(rep, 4))
        )

    def to_near(c):
        part = (slice(None), span(c))
        return send(
            near_out.at[part], near_in.at[part], n_send.at[c], n_recv.at[c], (me, flip(rep, 2))
        )

    def to_home(j, c):
        part = (j, span(c))
        return send(
            near.at[part], back.at[part], b_send.at[j, c], b_recv.at[j, c], (flip(me, j), rep)
        )

    def to_hbm(c):
        part = (slice(None), span(c))
        return pltpu.make_async_copy(back.at[part], buddy_hbm.at[part], store_sem.at[c])

    def bit(j, mask):
        return (offsets[j] // mask) % 2 == 1

    def staying(mask):
        index = jnp.int32(0)
        for j in reversed(range(groups)):
            index = jnp.where(bit(j, mask), index, j)
        return index

    stays_far, stays_near = staying(4), staying(2)

    def pack(here, out, stays, part):
        for i in range(groups - 1):
            out[i, part] = choose(stays <= i, here(i + 1), here(i))

    def unpack(here, arrived, stays, mask, target, part):
        for j in range(groups):
            if j == 0:
                theirs = arrived[0, part]
            elif j == groups - 1:
                theirs = arrived[j - 1, part]
            else:
                theirs = choose(stays < j, arrived[j - 1, part], arrived[j, part])
            target[j, part] = choose(bit(j, mask), theirs, here(j))

    def step(t, carry):
        @pl.when(t < PARTS)
        def _():
            to_twin(t).start()

        def stage(lag, work):
            c = t - lag

            @pl.when(jnp.logical_and(c >= 0, c < PARTS))
            def _():
                work(c)

        def leave(c):
            to_twin(c).wait_recv()
            part = span(c)
            for j in reversed(range(groups)):
                ready[j, part] = choose(bit(0, 1), twin[j, part], fresh[j, part])
                if j > 0:
                    to_guest(j, c).start()

        def visit(part):
            return lambda j: (ready if j == 0 else guest)[j, part]

        def cross_far(c):
            for j in others:
                to_guest(j, c).wait_recv()
            part = span(c)
            pack(visit(part), far_out, stays_far, part)
            to_far(c).start()

        def cross_near(c):
            to_far(c).wait_recv()
            part = span(c)
            unpack(visit(part), far_in, stays_far, 4, far, part)
            pack(lambda j: far[j, part], near_out, stays_near, part)
            to_near(c).start()

        def go_home(c):
            to_near(c).wait_recv()
            part = span(c)
            unpack(lambda j: far[j, part], near_in, stays_near, 2, near, part)
            for j in others:
                to_home(j, c).start()
            back[0, part] = near[0, part]

        def arrive(c):
            for j in others:
                to_home(j, c).wait_recv()
            to_hbm(c).start()

        stage(2, leave)
        stage(4, cross_far)
        stage(6, cross_near)
        stage(8, go_home)
        stage(10, arrive)
        return carry

    lax.fori_loop(0, 4, step, 0)
    homeward = Homeward(groups, targets, result, send_r, recv_r, r_send, r_recv)
    homeward.start()
    lax.fori_loop(4, PARTS, step, 0)
    homeward.finish(home)
    bring = pltpu.make_async_copy(home, precond_hbm, home_sem.at[0])
    bring.start()
    lax.fori_loop(PARTS, PARTS + 10, step, 0)
    bring.wait()
    homeward.wait_send()

    def drain(c, carry):
        to_twin(c).wait_send()
        to_far(c).wait_send()
        to_near(c).wait_send()
        for j in others:
            to_guest(j, c).wait_send()
            to_home(j, c).wait_send()
        to_hbm(c).wait()
        return carry

    lax.fori_loop(0, PARTS, drain, 0)


def hand_on(fresh, buddy, precond, nleft, nright, bleft, bright, home, stage, load_sem, store_sem):
    per = precond.shape[0]
    loads, stores = [], []
    pairs = [(fresh, 0, nleft), (fresh, per, nright), (buddy, 0, bleft), (buddy, per, bright)]
    for i, (source, first, target) in enumerate(pairs + [(precond, 0, home)]):
        for s in range(per):
            loads.append(
                pltpu.make_async_copy(source.at[first + s], stage.at[i, s], load_sem.at[i, s])
            )
            stores.append(
                pltpu.make_async_copy(stage.at[i, s], target.at[s], store_sem.at[i, s])
            )
    for load in loads:
        load.start()
    for load, store in zip(loads, stores):
        load.wait()
        store.start()
    for store in stores:
        store.wait()


def per_device(
    groups,
    replicas,
    grads,
    targets,
    left_factor,
    right_factor,
    left_root,
    right_root,
    refresh,
    buddy_offset,
):
    per, width = grads.shape[2], grads.shape[3]
    levels = replicas.bit_length() - 1
    chunks = 2 * per * CUTS
    shape = grads.shape
    blocks = (per, width, width)
    matrices = (2 * per, width, width)
    slots = (groups, width, width)
    bf = jnp.bfloat16
    smem = pl.BlockSpec(memory_space=pltpu.SMEM)
    vmem = pl.BlockSpec(memory_space=pltpu.VMEM)
    hbm = pl.BlockSpec(memory_space=pl.ANY)
    dma = pltpu.SemaphoreType.DMA

    def held(dims, kind=bf):
        return pltpu.VMEM(dims, kind)

    def params(number):
        return pltpu.CompilerParams(
            collective_id=number, has_side_effects=True, vmem_limit_bytes=56 * 1024 * 1024
        )

    table = targets.transpose(1, 2, 0).reshape(per, groups)
    fresh, result, offsets = pl.pallas_call(
        functools.partial(refresh_kernel, groups),
        out_shape=[
            jax.ShapeDtypeStruct(matrices, bf),
            jax.ShapeDtypeStruct(blocks, bf),
            jax.ShapeDtypeStruct((groups, 8, 128), jnp.int32),
        ],
        in_specs=[smem, smem, smem, vmem, hbm, hbm, hbm, hbm],
        out_specs=[hbm, hbm, vmem],
        scratch_shapes=[
            held(matrices, jnp.float32),
            held(matrices),
            held(matrices),
            held(matrices),
            held(slots),
            held(slots),
            held(blocks),
            held(matrices),
            held(blocks),
            held((groups, 8, 128), jnp.int32),
            dma((2, 2 * per)),
            dma((3 * per,)),
            dma((groups,)),
            dma((groups,)),
            dma((groups,)),
            dma((groups,)),
        ],
        compiler_params=params(0),
        name="refresh",
    )(
        table,
        refresh.reshape(per),
        buddy_offset,
        grads.reshape(blocks),
        left_factor.reshape(blocks),
        right_factor.reshape(blocks),
        left_root.reshape(blocks),
        right_root.reshape(blocks),
    )
    offsets = offsets[:, 0, 0]

    def finish(body, number, name, scratch):
        return pl.pallas_call(
            body,
            out_shape=[jax.ShapeDtypeStruct(matrices, bf), jax.ShapeDtypeStruct(blocks, bf)],
            in_specs=[smem, smem, vmem, vmem],
            out_specs=[hbm, hbm],
            scratch_shapes=[held(slots), held(slots), held(blocks)] + scratch,
            compiler_params=params(number),
            name=name,
        )

    butterfly = finish(
        functools.partial(butterfly_kernel, groups, replicas),
        1,
        "butterfly",
        [
            held((levels,) + matrices),
            dma((chunks,)),
            dma((1,)),
            dma((groups,)),
            dma((groups,)),
            dma((levels, chunks)),
            dma((levels, chunks)),
        ],
    )
    inputs = (offsets, table, fresh, result)
    if groups == 4 and replicas == 8 and 2 * per == groups:
        moving = (groups - 1, width, width)
        each = [dma((PARTS,)), dma((PARTS,))]
        pairs = [dma((groups, PARTS)), dma((groups, PARTS))]
        spread = finish(
            spread_kernel,
            2,
            "spread",
            [held(matrices)] * 3
            + [held(moving)] * 2
            + [held(matrices)]
            + [held(moving)] * 2
            + [held(matrices)] * 2
            + [dma((PARTS,)), dma((1,)), dma((groups,)), dma((groups,))]
            + each
            + pairs
            + each
            + each
            + pairs,
        )
        far = jnp.sum((offsets // 4) % 2)
        near = jnp.sum((offsets // 2) % 2)
        buddy, home = lax.cond(
            jnp.logical_and(far < groups, near < groups),
            lambda *ins: spread(*ins),
            lambda *ins: butterfly(*ins),
            *inputs,
        )
    else:
        buddy, home = butterfly(*inputs)
    outs = pl.pallas_call(
        hand_on,
        out_shape=[jax.ShapeDtypeStruct(blocks, bf)] * 5,
        in_specs=[hbm] * 3,
        out_specs=[hbm] * 5,
        scratch_shapes=[held((5,) + blocks), dma((5, per)), dma((5, per))],
        name="hand_on",
    )(fresh, buddy, home)
    return tuple(out.reshape(shape) for out in outs)


def solution(mesh):
    blocks = P("fsdp", "rep", None, None, None)
    placed = (
        blocks,
        P(None, "rep", None),
        blocks,
        blocks,
        blocks,
        blocks,
        P("fsdp", "rep", None),
        P("fsdp"),
    )
    return jax.shard_map(
        functools.partial(per_device, mesh.shape["fsdp"], mesh.shape["rep"]),
        mesh=mesh,
        in_specs=placed,
        out_specs=(blocks,) * 5,
        check_vma=False,
    )
```

time: 137 us -> 152 us (1.11); the launches traced: 135 us -> 152 us
  Pallas kernels: 134 us -> 148 us
    pallas_call x1 -> x2, Pallas kernels: 129 us -> 144 us  [the longest x1 107 us: per_device(): spread(*ins)]
where the time goes in v4:
time: 152 us
  Pallas kernels  148 us (97%)
  between operations  2.62 us (2%)
    pallas_call x1, Pallas kernels, per_device(): spread(*ins)  107 us
    pallas_call x1, Pallas kernels, per_device(): pl.pallas_call(functools.partial(refresh_kernel, groups), out_shape=[jax....  36.5 us
    pallas_call x1, Pallas kernels, per_device(): pl.pallas_call(hand_on, out_shape=[jax.ShapeDtypeStruct(blocks, bf)] * 5,...  3.9 us

profile of v4, /device:TPU:0, one launch (start us, length us, event | category | flops | bytes accessed | tf_op | source)
XLA Modules:
  0.0 151.9 jit_solution(8802268939014344800)
XLA Ops:
  1.3 0.0 copy-start
  1.3 36.5 %refresh.1 = (bf16[4,512,512]{2,1,0:T(8,128)(2,1)S(1)}, bf16[2,512,512]{2,1,0:T(8,128)(2,1)S(1)}, s32[4,8,128]{2,1,0:T(8,128)}) custom-call(s32[2,4]{1,0:T(2,128)} %bitcast.19, s32[2]{0:T(128)} %bitcast.22, s32[1]{0:T(128)S(6)} %copy.17.offset, bf16[2,512,512]{2,1,0:T(8,128)(2,1)} %bitcast.16, f32[2,512,512]{2,1,0:T(8,128)} %bitcast.14, ...), custom_call_target="tpu_custom_call" | custom-call | tf_op jit(solution)/shard_map/refresh/pallas_call | solution.py:570
  37.8 0.9 slice_reduce_fusion
  38.7 0.7 fusion.1
  40.6 0.0 copy-done
  40.6 107.3 %conditional.1 = ((bf16[4,512,512]{2,1,0:T(8,128)(2,1)}, bf16[2,512,512]{2,1,0:T(8,128)(2,1)})) conditional(s32[]{:T(128)} %convert_element_type.3, (s32[4]{0:T(128)S(1)}, s32[2,4]{1,0:T(2,128)S(1)}, bf16[4,512,512]{2,1,0:T(8,128)(2,1)S(1)}, bf16[2,512,512]{2,1,0:T(8,128)(2,1)S(1)}) %tuple.21, (s32[4]{0:T(128)S(1)}, s32[2,4]{1,0:T(2,128)S(1)}, ...), branch_computations={%region_2.3_spmd, %region_3.4_spmd} | conditional | bytes 8 | solution.py:659
  40.7 107.3 %spread.1 = (bf16[4,512,512]{2,1,0:T(8,128)(2,1)}, bf16[2,512,512]{2,1,0:T(8,128)(2,1)}) custom-call(s32[4]{0:T(128)S(1)} %get-tuple-element.20.offsets, s32[2,4]{1,0:T(2,128)S(1)} %get-tuple-element.21.targets, bf16[4,512,512]{2,1,0:T(8,128)(2,1)S(1)} %get-tuple-element.22.fresh, bf16[2,512,512]{2,1,0:T(8,128)(2,1)S(1)} %get-tuple-element.23.result), custom_call_target="tpu_custom_call" | custom-call | tf_op jit(solution)/shard_map/cond/branch_1_fun/spread/pallas_call | solution.py:661
  148.0 3.9 %hand_on.1 = (bf16[2,512,512]{2,1,0:T(8,128)(2,1)}, bf16[2,512,512]{2,1,0:T(8,128)(2,1)}, bf16[2,512,512]{2,1,0:T(8,128)(2,1)}, bf16[2,512,512]{2,1,0:T(8,128)(2,1)}, bf16[2,512,512]{2,1,0:T(8,128)(2,1)}) custom-call(bf16[4,512,512]{2,1,0:T(8,128)(2,1)S(1)} %get-tuple-element.39.fresh, bf16[4,512,512]{2,1,0:T(8,128)(2,1)} %get-tuple-element.42.buddy, ...), custom_call_target="tpu_custom_call" | custom-call | tf_op jit(solution)/shard_map/hand_on/pallas_call | solution.py:667
Async XLA Ops:
  1.3 39.4 %copy-start = (s32[4,1,2]{0,2,1:T(2,128)S(1)}, s32[4,1,2]{0,2,1:T(2,128)}, u32[]{:S(2)}) copy-start(s32[4,1,2]{0,2,1:T(2,128)} %param.11) | copy-start | bytes 100

commit v5 on v3

--- a/solution.py
+++ b/solution.py
@@ -43,7 +43,7 @@
     targets,
     refresh,
     offset,
-    grads,
+    grads_hbm,
     lfac_hbm,
     rfac_hbm,
     lroot_hbm,
@@ -53,6 +53,7 @@
     bleft_hbm,
     bright_hbm,
     precond_hbm,
+    grads,
     fac,
     root,
     fifth_hi,
@@ -83,6 +84,17 @@
     rows = width // CUTS
     chunks = 2 * per * CUTS
 
+    blocks_in = pltpu.make_async_copy(grads_hbm, grads, in_sem.at[2, 0])
+    blocks_in.start()
+
+    barrier = pltpu.get_barrier_semaphore()
+    for j in range(1, groups):
+        pl.semaphore_signal(barrier, inc=1, device_id=(flip(me, j), rep), device_id_type=MESH)
+    for level in range(levels):
+        pl.semaphore_signal(
+            barrier, inc=1, device_id=(me, flip(rep, 1 << level)), device_id_type=MESH
+        )
+
     loads = []
     for s in range(per):
         for side, (f_hbm, x_hbm) in enumerate(((lfac_hbm, lroot_hbm), (rfac_hbm, rroot_hbm))):
@@ -92,14 +104,6 @@
     for load in loads:
         load.start()
 
-    barrier = pltpu.get_barrier_semaphore()
-    for j in range(1, groups):
-        pl.semaphore_signal(barrier, inc=1, device_id=(flip(me, j), rep), device_id_type=MESH)
-    for level in range(levels):
-        pl.semaphore_signal(
-            barrier, inc=1, device_id=(me, flip(rep, 1 << level)), device_id_type=MESH
-        )
-
     def block_for(owner):
         index = jnp.int32(0)
         for k in range(1, per):
@@ -107,10 +111,6 @@
         return index
 
     order = sorted(range(1, groups), key=lambda j: -bin(j).count("1"))
-    for j in order:
-        send_g[j] = grads[block_for(flip(me, j))]
-    pl.semaphore_wait(barrier, groups - 1 + levels)
-
     def exchange(source, target, send_sem, recv_sem, j):
         return pltpu.make_async_remote_copy(
             src_ref=source.at[j],
@@ -122,7 +122,11 @@
         )
 
     outward = [exchange(send_g, recv_g, g_send, g_recv, j) for j in order]
-    for copy in outward:
+    blocks_in.wait()
+    for number, (j, copy) in enumerate(zip(order, outward)):
+        send_g[j] = grads[block_for(flip(me, j))]
+        if number == 0:
+            pl.semaphore_wait(barrier, groups - 1 + levels)
         copy.start()
     recv_g[0] = grads[block_for(me)]
     for load in loads:
@@ -135,6 +139,7 @@
         hi, lo = split(mm(x, fourth[0]) + mm(x, fourth[1]))
         fifth_hi[m] = hi
         fifth_lo[m] = lo
+        fac[m] = (5.0 * x.astype(jnp.float32) - mm3((hi, lo), split(fac[m]))) / 4.0
         return carry
 
     lax.fori_loop(0, 2 * per, powers, 0)
@@ -162,29 +167,34 @@
             device_id_type=MESH,
         )
 
-    def newton(m, s, gram):
-        factor = split(fac[m] + gram)
-        moment = mm3((fifth_hi[m], fifth_lo[m]), factor)
-        old = root[m].astype(jnp.float32)
-        new = (5.0 * old - moment) / 4.0
-        fresh[m] = jnp.where(refresh[s] == 1, new, old).astype(jnp.bfloat16)
+    def along(left, right, dim):
+        return lax.dot_general(
+            left, right, (((1,), (dim,)), ((), ())), preferred_element_type=jnp.float32
+        )
+
+    def newton(m, s, block, first, count):
+        part = pl.ds(first, count)
+        near, far = (0, 1) if m % 2 == 0 else (1, 0)
+        upper = along(fifth_hi[m, part], block, near) + along(fifth_lo[m, part], block, near)
+        high, low = split(upper)
+        moment = along(high, block, far) + along(low, block, far)
+        new = fac[m, part] - moment / 4.0
+        old = root[m, part].astype(jnp.float32)
+        fresh[m, part] = jnp.where(refresh[s] == 1, new, old).astype(jnp.bfloat16)
 
     stores = []
     for s in range(per):
         block = owned[s]
-        newton(
-            2 * s,
-            s,
-            lax.dot_general(block, block, (((1,), (1,)), ((), ())), preferred_element_type=jnp.float32),
-        )
         if s == 0:
-            for c in range(AHEAD):
+            newton(0, 0, block, 0, AHEAD // 2 * rows)
+            for c in range(AHEAD // 2):
                 buddy_copy(0, c).start()
-        newton(
-            2 * s + 1,
-            s,
-            lax.dot_general(block, block, (((0,), (0,)), ((), ())), preferred_element_type=jnp.float32),
-        )
+            newton(0, 0, block, AHEAD // 2 * rows, width - AHEAD // 2 * rows)
+            for c in range(AHEAD // 2, AHEAD):
+                buddy_copy(0, c).start()
+        else:
+            newton(2 * s, s, block, 0, width)
+        newton(2 * s + 1, s, block, 0, width)
         half = mm(fresh[2 * s], block).astype(jnp.bfloat16)
         result[s] = mm(half, fresh[2 * s + 1]).astype(jnp.bfloat16)
         for side, out in enumerate((nleft_hbm, nright_hbm)):
@@ -315,7 +325,6 @@
     blocks = (per, width, width)
     bf = jnp.bfloat16
     smem = pl.BlockSpec(memory_space=pltpu.SMEM)
-    vmem = pl.BlockSpec(memory_space=pltpu.VMEM)
     hbm = pl.BlockSpec(memory_space=pl.ANY)
     dma = pltpu.SemaphoreType.DMA
     matrices = (2 * per, width, width)
@@ -324,9 +333,10 @@
     outs = pl.pallas_call(
         functools.partial(kernel, groups, replicas),
         out_shape=[jax.ShapeDtypeStruct(blocks, bf)] * 5,
-        in_specs=[smem, smem, smem, vmem, hbm, hbm, hbm, hbm],
+        in_specs=[smem, smem, smem, hbm, hbm, hbm, hbm, hbm],
         out_specs=[hbm] * 5,
         scratch_shapes=[
+            pltpu.VMEM(blocks, bf),
             pltpu.VMEM(matrices, jnp.float32),
             pltpu.VMEM(matrices, bf),
             pltpu.VMEM(matrices, bf),
@@ -340,7 +350,7 @@
             pltpu.VMEM(slots, bf),
             pltpu.VMEM(blocks, bf),
             pltpu.VMEM((levels,) + matrices, bf),
-            dma((2, 2 * per)),
+            dma((3, 2 * per)),
             dma((2 * per + 1,)),
             dma((chunks,)),
             dma((groups,)),

time: 137 us -> 136 us (level)
  no operation moved by 1% of the time
where the time goes in v5:
time: 136 us; the launch traced here: 135 us
  Pallas kernels  134 us (99%)
    pallas_call x1, Pallas kernels, per_device(): pl.pallas_call(functools.partial(kernel, groups, replicas), out_shape=[ja...  129 us
    pallas_call x1, Pallas kernels, per_device(): pl.pallas_call(hand_on, out_shape=[jax.ShapeDtypeStruct(blocks, bf)] * 5,...  4.71 us

profile of v5, /device:TPU:0, one launch (start us, length us, event | category | flops | bytes accessed | tf_op | source)
XLA Modules:
  0.0 135.4 jit_solution(3380465896010169154)
XLA Ops:
  1.3 129.4 %refresh_and_exchange.1 = (bf16[2,512,512]{2,1,0:T(8,128)(2,1)}, bf16[2,512,512]{2,1,0:T(8,128)(2,1)}, bf16[2,512,512]{2,1,0:T(8,128)(2,1)}, bf16[2,512,512]{2,1,0:T(8,128)(2,1)}, bf16[2,512,512]{2,1,0:T(8,128)(2,1)}) custom-call(s32[2,4]{1,0:T(2,128)} %bitcast.24, s32[2]{0:T(128)} %bitcast.25, s32[1]{0:T(128)S(6)} %copy.13.offset, ...), custom_call_target="tpu_custom_call" | custom-call | flops 11811160064 | bytes 12582912 | tf_op jit(solution)/shard_map/refresh_and_exchange/pallas_call | solution.py:333
  130.7 4.7 %hand_on.1 = (bf16[2,512,512]{2,1,0:T(8,128)(2,1)}, bf16[2,512,512]{2,1,0:T(8,128)(2,1)}, bf16[2,512,512]{2,1,0:T(8,128)(2,1)}, bf16[2,512,512]{2,1,0:T(8,128)(2,1)}, bf16[2,512,512]{2,1,0:T(8,128)(2,1)}) custom-call(bf16[2,512,512]{2,1,0:T(8,128)(2,1)} %get-tuple-element.15.refs_0_, bf16[2,512,512]{2,1,0:T(8,128)(2,1)} %get-tuple-element.16.refs_1_, ...), custom_call_target="tpu_custom_call" | custom-call | tf_op jit(solution)/shard_map/hand_on/pallas_call | solution.py:380

commit v6 on v5

--- a/solution.py
+++ b/solution.py
@@ -11,6 +11,7 @@
 CUTS = 8
 AHEAD = 4
 BEHIND = 3
+KEPT = 4
 
 
 def flip(index, mask):
@@ -48,10 +49,8 @@
     rfac_hbm,
     lroot_hbm,
     rroot_hbm,
-    nleft_hbm,
-    nright_hbm,
-    bleft_hbm,
-    bright_hbm,
+    fresh_hbm,
+    buddy_hbm,
     precond_hbm,
     grads,
     fac,
@@ -197,9 +196,8 @@
         newton(2 * s + 1, s, block, 0, width)
         half = mm(fresh[2 * s], block).astype(jnp.bfloat16)
         result[s] = mm(half, fresh[2 * s + 1]).astype(jnp.bfloat16)
-        for side, out in enumerate((nleft_hbm, nright_hbm)):
-            m = 2 * s + side
-            stores.append(pltpu.make_async_copy(fresh.at[m], out.at[s], out_sem.at[m]))
+        for m in (2 * s, 2 * s + 1):
+            stores.append(pltpu.make_async_copy(fresh.at[m], fresh_hbm.at[m], out_sem.at[m]))
             stores[-1].start()
 
     for j in [0] + order:
@@ -215,21 +213,12 @@
     for copy in backward:
         copy.start()
 
-    def buddy_store(c, wait):
-        s, cut = c // (2 * CUTS), pl.multiple_of((c % CUTS) * rows, rows)
-        for side, out in enumerate((bleft_hbm, bright_hbm)):
-
-            @pl.when((c // CUTS) % 2 == side)
-            def _():
-                copy = pltpu.make_async_copy(
-                    moved.at[levels - 1, 2 * s + side, pl.ds(cut, rows)],
-                    out.at[s, pl.ds(cut, rows)],
-                    buddy_out_sem.at[c],
-                )
-                if wait:
-                    copy.wait()
-                else:
-                    copy.start()
+    def buddy_store(c):
+        m, cut = c // CUTS, pl.multiple_of((c % CUTS) * rows, rows)
+        part = (m, pl.ds(cut, rows))
+        return pltpu.make_async_copy(
+            moved.at[levels - 1].at[part], buddy_hbm.at[part], buddy_out_sem.at[c]
+        )
 
     def step(t, carry):
         @pl.when(t < chunks)
@@ -254,7 +243,13 @@
                 if n < levels - 1:
                     buddy_copy(n + 1, c).start()
                 else:
-                    buddy_store(c, False)
+                    buddy_store(c).start()
+                    for earlier in range(levels):
+                        buddy_copy(earlier, c).wait_send()
+
+                    @pl.when(c >= KEPT)
+                    def _():
+                        buddy_store(c - KEPT).wait()
 
         return carry
 
@@ -277,25 +272,22 @@
     for copy in outward + backward:
         copy.wait_send()
 
-    def drain(c, carry):
-        for n in range(levels):
-            buddy_copy(n, c).wait_send()
-        buddy_store(c, True)
-        return carry
-
-    lax.fori_loop(0, chunks, drain, 0)
-
-
-def hand_on(*refs):
-    sources, targets, (stage, load_sem, store_sem) = refs[:5], refs[5:10], refs[10:]
+    for c in range(chunks - KEPT, chunks):
+        buddy_store(c).wait()
+
+
+def hand_on(fresh, buddy, precond, nleft, nright, bleft, bright, home, stage, load_sem, store_sem):
+    per = precond.shape[0]
     loads, stores = [], []
-    for i in range(5):
-        for s in range(sources[i].shape[0]):
+    plan = [(fresh, 0, nleft), (fresh, 1, nright), (buddy, 0, bleft), (buddy, 1, bright)]
+    for i, (source, side, target) in enumerate(plan + [(precond, None, home)]):
+        for s in range(per):
+            block = s if side is None else 2 * s + side
             loads.append(
-                pltpu.make_async_copy(sources[i].at[s], stage.at[i, s], load_sem.at[i, s])
+                pltpu.make_async_copy(source.at[block], stage.at[i, s], load_sem.at[i, s])
             )
             stores.append(
-                pltpu.make_async_copy(stage.at[i, s], targets[i].at[s], store_sem.at[i, s])
+                pltpu.make_async_copy(stage.at[i, s], target.at[s], store_sem.at[i, s])
             )
     for load in loads:
         load.start()
@@ -332,9 +324,9 @@
     products = 2 * per * 10 + 2 * per
     outs = pl.pallas_call(
         functools.partial(kernel, groups, replicas),
-        out_shape=[jax.ShapeDtypeStruct(blocks, bf)] * 5,
+        out_shape=[jax.ShapeDtypeStruct(dims, bf) for dims in (matrices, matrices, blocks)],
         in_specs=[smem, smem, smem, hbm, hbm, hbm, hbm, hbm],
-        out_specs=[hbm] * 5,
+        out_specs=[hbm] * 3,
         scratch_shapes=[
             pltpu.VMEM(blocks, bf),
             pltpu.VMEM(matrices, jnp.float32),
@@ -380,7 +372,7 @@
     outs = pl.pallas_call(
         hand_on,
         out_shape=[jax.ShapeDtypeStruct(blocks, bf)] * 5,
-        in_specs=[hbm] * 5,
+        in_specs=[hbm] * 3,
         out_specs=[hbm] * 5,
         scratch_shapes=[pltpu.VMEM((5,) + blocks, bf), dma((5, per)), dma((5, per))],
         name="hand_on",

time: 136 us -> 136 us (level)
  no operation moved by 1% of the time
where the time goes in v6:
time: 136 us; the launch traced here: 135 us
  Pallas kernels  134 us (99%)
    pallas_call x1, Pallas kernels, per_device(): pl.pallas_call(functools.partial(kernel, groups, replicas), out_shape=[ja...  129 us
    pallas_call x1, Pallas kernels, per_device(): pl.pallas_call(hand_on, out_shape=[jax.ShapeDtypeStruct(blocks, bf)] * 5,...  4.71 us

profile of v6, /device:TPU:0, one launch (start us, length us, event | category | flops | bytes accessed | tf_op | source)
XLA Modules:
  0.0 135.5 jit_solution(4292344139012592257)
XLA Ops:
  1.3 129.5 %refresh_and_exchange.1 = (bf16[4,512,512]{2,1,0:T(8,128)(2,1)}, bf16[4,512,512]{2,1,0:T(8,128)(2,1)}, bf16[2,512,512]{2,1,0:T(8,128)(2,1)}) custom-call(s32[2,4]{1,0:T(2,128)} %bitcast.24, s32[2]{0:T(128)} %bitcast.25, s32[1]{0:T(128)S(6)} %copy.13.offset, bf16[2,512,512]{2,1,0:T(8,128)(2,1)} %bitcast.16, f32[2,512,512]{2,1,0:T(8,128)} %bitcast.14, ...), custom_call_target="tpu_custom_call" | custom-call | flops 11811160064 | bytes 12582912 | tf_op jit(solution)/shard_map/refresh_and_exchange/pallas_call | solution.py:325
  130.7 4.7 %hand_on.1 = (bf16[2,512,512]{2,1,0:T(8,128)(2,1)}, bf16[2,512,512]{2,1,0:T(8,128)(2,1)}, bf16[2,512,512]{2,1,0:T(8,128)(2,1)}, bf16[2,512,512]{2,1,0:T(8,128)(2,1)}, bf16[2,512,512]{2,1,0:T(8,128)(2,1)}) custom-call(bf16[4,512,512]{2,1,0:T(8,128)(2,1)} %get-tuple-element.13.fresh, bf16[4,512,512]{2,1,0:T(8,128)(2,1)} %get-tuple-element.14.buddy, ...), custom_call_target="tpu_custom_call" | custom-call | tf_op jit(solution)/shard_map/hand_on/pallas_call | solution.py:372

commit v7 on v6

--- a/solution.py
+++ b/solution.py
@@ -9,8 +9,8 @@
 
 MESH = pl.DeviceIdType.MESH
 CUTS = 8
-AHEAD = 4
-BEHIND = 3
+AHEAD = 6
+BEHIND = 4
 KEPT = 4
 
 
@@ -153,8 +153,16 @@
                 place = jnp.where(targets[k, source] == me * per + s, j, place)
         owned[s] = recv_g[place]
 
+    def routes(level_no):
+        level = levels - 1 - level_no
+        if levels > 1 and level_no < 2:
+            return level, 2 * levels - 3 - level
+        return level, level
+
     def buddy_copy(level_no, c):
-        level = levels - 1 - level_no
+        even, odd = routes(level_no)
+        turn = c % 2
+        device = flip(rep, 1 << even) * (1 - turn) + flip(rep, 1 << odd) * turn
         source = fresh if level_no == 0 else moved.at[level_no - 1]
         m, cut = c // CUTS, pl.multiple_of((c % CUTS) * rows, rows)
         return pltpu.make_async_remote_copy(
@@ -162,7 +170,7 @@
             dst_ref=moved.at[level_no, m, pl.ds(cut, rows)],
             send_sem=b_send.at[level_no, c],
             recv_sem=b_recv.at[level_no, c],
-            device_id=(me, flip(rep, 1 << level)),
+            device_id=(me, device),
             device_id_type=MESH,
         )
 
@@ -232,8 +240,8 @@
             def _():
                 buddy_copy(n, c).wait_recv()
                 m, cut = c // CUTS, pl.multiple_of((c % CUTS) * rows, rows)
-                level = levels - 1 - n
-                crossing = (offset[0] // (1 << level)) % 2 == 1
+                even, odd = [(offset[0] // (1 << level)) % 2 for level in routes(n)]
+                crossing = jnp.where(c % 2 == 0, even, odd) == 1
                 here = fresh if n == 0 else moved.at[n - 1]
                 mine = here[m, pl.ds(cut, rows)].astype(jnp.float32)
                 theirs = moved[n, m, pl.ds(cut, rows)].astype(jnp.float32)

time: 136 us -> 132 us (0.971)
  Pallas kernels: 134 us -> 130 us
    pallas_call x1, Pallas kernels: 129 us -> 125 us  [per_device(): pl.pallas_call(functools.partial(kernel, groups, replicas), out_shape=[ja...]
where the time goes in v7:
time: 132 us; the launch traced here: 131 us
  Pallas kernels  130 us (98%)
    pallas_call x1, Pallas kernels, per_device(): pl.pallas_call(functools.partial(kernel, groups, replicas), out_shape=[ja...  125 us
    pallas_call x1, Pallas kernels, per_device(): pl.pallas_call(hand_on, out_shape=[jax.ShapeDtypeStruct(blocks, bf)] * 5,...  4.71 us

profile of v7, /device:TPU:0, one launch (start us, length us, event | category | flops | bytes accessed | tf_op | source)
XLA Modules:
  0.0 131.3 jit_solution(9753454325059585179)
XLA Ops:
  1.3 125.3 %refresh_and_exchange.1 = (bf16[4,512,512]{2,1,0:T(8,128)(2,1)}, bf16[4,512,512]{2,1,0:T(8,128)(2,1)}, bf16[2,512,512]{2,1,0:T(8,128)(2,1)}) custom-call(s32[2,4]{1,0:T(2,128)} %bitcast.24, s32[2]{0:T(128)} %bitcast.25, s32[1]{0:T(128)S(6)} %copy.13.offset, bf16[2,512,512]{2,1,0:T(8,128)(2,1)} %bitcast.16, f32[2,512,512]{2,1,0:T(8,128)} %bitcast.14, ...), custom_call_target="tpu_custom_call" | custom-call | flops 11811160064 | bytes 12582912 | tf_op jit(solution)/shard_map/refresh_and_exchange/pallas_call | solution.py:333
  126.6 4.7 %hand_on.1 = (bf16[2,512,512]{2,1,0:T(8,128)(2,1)}, bf16[2,512,512]{2,1,0:T(8,128)(2,1)}, bf16[2,512,512]{2,1,0:T(8,128)(2,1)}, bf16[2,512,512]{2,1,0:T(8,128)(2,1)}, bf16[2,512,512]{2,1,0:T(8,128)(2,1)}) custom-call(bf16[4,512,512]{2,1,0:T(8,128)(2,1)} %get-tuple-element.13.fresh, bf16[4,512,512]{2,1,0:T(8,128)(2,1)} %get-tuple-element.14.buddy, ...), custom_call_target="tpu_custom_call" | custom-call | tf_op jit(solution)/shard_map/hand_on/pallas_call | solution.py:380
